TPU v7x, 32 devices: a whole 2x2x4 slice. The times are simulated.
32 devices in a mesh: groups: 2 (over x), replica: 4 (over z), tensor: 4 (over y, core).
Axes of the slice: x: 2, y: 2, z: 4, core: 2. Of those that a mesh axis runs over, the one named last changes fastest.
Arguments:
- hidden_input: bfloat16 [512, 8192], P(('groups', 'replica'), 'tensor'), parts along dimension 0, may hold values from -6 to 6
- norm_gain_vector: float32 [8192], replicated, may hold values from 0.5 to 1.5
- query_weight: bfloat16 [8192, 4096], P(None, 'tensor'), may hold values from -0.0625 to 0.0625
- key_weight: bfloat16 [8192, 512], P(None, 'tensor'), may hold values from -0.0625 to 0.0625
- value_weight: bfloat16 [8192, 512], P(None, 'tensor'), may hold values from -0.0625 to 0.0625
- output_weight: bfloat16 [4096, 8192], P('tensor'), may hold values from -0.09375 to 0.09375
- key_cache_rows: bfloat16 [512, 64, 512], P(('groups', 'replica', 'tensor')), parts along dimension 0, may hold values from -95 to 95
- value_cache_rows: bfloat16 [512, 64, 512], P(('groups', 'replica', 'tensor')), parts along dimension 0, may hold values from -6 to 6
- cache_length: int32 [512], P(('groups', 'replica', 'tensor')), parts along dimension 0, may hold values from 1 to 64, as said below
- adapter_index: int32 [512], P(('groups', 'replica')), parts along dimension 0, may hold values from 0 to 63
- query_down_weight: bfloat16 [128, 8192, 16], P(('groups', 'replica'), 'tensor'), parts along dimension 0, may hold values from -0.0625 to 0.0625
- query_up_weight: bfloat16 [128, 16, 4096], P(('groups', 'replica'), None, 'tensor'), parts along dimension 0, may hold values from -1.5 to 1.5
- output_down_weight: bfloat16 [128, 4096, 16], P(('groups', 'replica'), 'tensor'), parts along dimension 0, may hold values from -0.09375 to 0.09375
- output_up_weight: bfloat16 [128, 16, 8192], P(('groups', 'replica'), None, 'tensor'), parts along dimension 0, may hold values from -1.5 to 1.5
Outputs:
- mixed: bfloat16 [512, 8192], P(('groups', 'replica'), 'tensor'), parts along dimension 0
There are 2 independent parts, one for each index of `groups`. A program takes and returns all parts, laid end to end along the dimension named above; an argument that names none is the same for every part. Nothing has to cross between parts.
Inputs may be any that keep to these rules, and one draw needn't show every extreme that they name: `cache_length`: every request holds at least one live slot; some request holds all 64.
All inputs are finite; a program needn't handle non-finite values.
Results may differ from a plain program's by a relative error of at most 0.0065.
The roundings to bfloat16 on the way count: a program that leaves them out, or rounds other values in their place, can miss the bound.
Values may be sent and summed in bfloat16 or wider, within the bound.
A program may use at most 128 MiB of HBM per device.

v0:
```python
import jax
import jax.numpy as jnp
from jax import lax
from jax.sharding import PartitionSpec as P

QUERY_HEADS = 32
KV = 4
HEAD_SIZE = 128
L = 64


ADAPTER_SCALE = 2.0
ROPE_BASE = 500000.0
EPSILON = 1e-05


def rotate(values, position):
    half = values.shape[-1] // 2
    freq = ROPE_BASE ** (-(jnp.arange(half, dtype=jnp.float32) / half))
    angle = position[:, None, None] * freq[None, None, :]
    first = values[..., :half]
    second = values[..., half:]
    cosine = jnp.cos(angle)
    sine = jnp.sin(angle)
    return jnp.concatenate(
        [first * cosine - second * sine, second * cosine + first * sine], axis=-1
    )


def attend(query_vectors, key_new, value_new, key_cache_rows, value_cache_rows, cache_length):
    count = query_vectors.shape[0]
    group = QUERY_HEADS // KV
    position = cache_length.astype(jnp.float32)
    rot_query = rotate(
        query_vectors.astype(jnp.float32).reshape(count, QUERY_HEADS, HEAD_SIZE), position
    ).astype(jnp.bfloat16)
    rotated_key = rotate(
        key_new.astype(jnp.float32).reshape(count, KV, HEAD_SIZE), position
    ).astype(jnp.bfloat16)
    grouped_query = rot_query.reshape(count, KV, group, HEAD_SIZE)
    keys = key_cache_rows.reshape(count, L, KV, HEAD_SIZE)
    values = value_cache_rows.reshape(count, L, KV, HEAD_SIZE)
    softmax_factor = 1.0 / HEAD_SIZE**0.5
    scores = (
        jnp.einsum("bkgd,blkd->bkgl", grouped_query, keys, preferred_element_type=jnp.float32)
        * softmax_factor
    )
    live = jnp.arange(L)[None, :] < cache_length[:, None]
    scores = jnp.where(live[:, None, None, :], scores, -1e30)
    own_scores = (
        jnp.einsum("enxs,ens->enx", grouped_query, rotated_key, preferred_element_type=jnp.float32)
        * softmax_factor
    )
    top = jnp.maximum(jnp.max(scores, axis=-1), own_scores)
    weights = jnp.exp(scores - top[..., None])
    weight_new = jnp.exp(own_scores - top)
    total = jnp.sum(weights, axis=-1) + weight_new
    probs = (weights / total[..., None]).astype(jnp.bfloat16)
    prob_new = (weight_new / total).astype(jnp.bfloat16)
    context_vectors = jnp.einsum(
        "bkgl,blkd->bkgd", probs, values, preferred_element_type=jnp.float32
    )
    fresh = value_new.reshape(count, KV, 1, HEAD_SIZE).astype(jnp.float32)
    context_vectors = context_vectors + prob_new[..., None].astype(jnp.float32) * fresh
    return context_vectors.astype(jnp.bfloat16).reshape(count, QUERY_HEADS * HEAD_SIZE)


def down_fetch(act, table, adapter_index):
    piece = lax.all_gather(table, "replica", axis=0, tiled=True)
    count = piece.shape[0]
    picked = adapter_index[:, None] == jnp.arange(count)[None, :]
    projected = jnp.einsum("rd,adk->rak", act, piece, preferred_element_type=jnp.float32)
    return jnp.sum(jnp.where(picked[:, :, None], projected, 0.0), axis=1)


def up_fetch(low, table, adapter_index):
    rank = table.shape[1]
    piece = lax.all_gather(table, "replica", axis=0, tiled=True)
    count = piece.shape[0]
    picked = adapter_index[:, None] == jnp.arange(count)[None, :]
    spread = jnp.where(picked[:, :, None], low[:, None, :], jnp.zeros((), jnp.bfloat16))
    spread = spread.reshape(low.shape[0], count * rank)
    return jnp.dot(
        spread, piece.reshape(count * rank, piece.shape[2]), preferred_element_type=jnp.float32
    )


def adapter_contribution(act, table_down, table_up, adapter_index):
    partial_low = down_fetch(act, table_down, adapter_index)
    low = lax.psum(partial_low, "tensor").astype(jnp.bfloat16)
    return up_fetch(low, table_up, adapter_index)


def per_device(
    hidden_input,
    norm_gain_vector,
    query_weight,
    key_weight,
    value_weight,
    output_weight,
    key_cache_rows,
    value_cache_rows,
    cache_length,
    adapter_index,
    query_down_weight,
    query_up_weight,
    output_down_weight,
    output_up_weight,
):
    width_local = hidden_input.shape[1]
    whole = lax.all_gather(hidden_input, "tensor", axis=1, tiled=True)
    residual_stream = whole.astype(jnp.float32)
    scale = lax.rsqrt(jnp.mean(residual_stream * residual_stream, axis=-1, keepdims=True) + EPSILON)
    normed_hidden = (residual_stream * scale * norm_gain_vector).astype(jnp.bfloat16)
    query_base = jnp.dot(normed_hidden, query_weight, preferred_element_type=jnp.float32)
    key_new = jnp.dot(normed_hidden, key_weight, preferred_element_type=jnp.float32).astype(
        jnp.bfloat16
    )
    value_new = jnp.dot(normed_hidden, value_weight, preferred_element_type=jnp.float32).astype(
        jnp.bfloat16
    )
    normed_portion = lax.dynamic_slice_in_dim(
        normed_hidden, lax.axis_index("tensor") * width_local, width_local, 1
    )
    query_vectors = (
        query_base
        + ADAPTER_SCALE
        * adapter_contribution(normed_portion, query_down_weight, query_up_weight, adapter_index)
    ).astype(jnp.bfloat16)
    q_rows, k_rows, v_rows = (
        lax.all_to_all(query_vectors, "tensor", split_axis=0, concat_axis=1, tiled=True),
        lax.all_to_all(key_new, "tensor", split_axis=0, concat_axis=1, tiled=True),
        lax.all_to_all(value_new, "tensor", split_axis=0, concat_axis=1, tiled=True),
    )
    context_vectors = attend(q_rows, k_rows, v_rows, key_cache_rows, value_cache_rows, cache_length)
    context_local = lax.all_to_all(
        context_vectors, "tensor", split_axis=1, concat_axis=0, tiled=True
    )
    base_projection = jnp.dot(context_local, output_weight, preferred_element_type=jnp.float32)
    base_portion = lax.psum_scatter(base_projection, "tensor", scatter_dimension=1, tiled=True)
    extra_output = adapter_contribution(
        context_local, output_down_weight, output_up_weight, adapter_index
    )
    return (hidden_input.astype(jnp.float32) + base_portion + ADAPTER_SCALE * extra_output).astype(
        jnp.bfloat16
    )


def solution(mesh):
    placed = (
        P(("groups", "replica"), "tensor"),
        P(),
        P(None, "tensor"),
        P(None, "tensor"),
        P(None, "tensor"),
        P("tensor", None),
        P(("groups", "replica", "tensor"), None, None),
        P(("groups", "replica", "tensor"), None, None),
        P(("groups", "replica", "tensor")),
        P(("groups", "replica")),
        P(("groups", "replica"), "tensor", None),
        P(("groups", "replica"), None, "tensor"),
        P(("groups", "replica"), "tensor", None),
        P(("groups", "replica"), None, "tensor"),
    )
    return jax.shard_map(
        per_device,
        mesh=mesh,
        in_specs=placed,
        out_specs=P(("groups", "replica"), "tensor"),
        check_vma=False,
    )
```

profile of v0, /device:TPU:0, one launch (start us, length us, event | category | flops | bytes accessed | tf_op | source)
XLA Modules:
  0.0 326.9 jit_solution(10771656557330330509)
XLA Ops:
  6.5 0.0 copy-start
  6.5 0.0 copy-start.3
  6.5 0.0 all-gather.6.cloned.1.call-start
  6.5 0.7 all-gather.6.cloned.1.call-update
  7.3 0.0 all-gather.8.cloned.1.call-start
  7.3 0.7 all-gather.8.cloned.1.call-update
  8.0 0.0 all-gather.10.cloned.1.call-start
  8.1 2.1 copy.28
  10.2 0.0 copy-start.5
  10.2 0.0 all-gather.10.cloned.1.call-update
  10.2 0.0 all-gather.12.cloned.1.call-start
  10.3 0.5 all-gather.12.cloned.1.call-update
  10.8 0.0 copy-start.4
  10.8 0.0 all-gather.14.cloned.1.call-start
  10.8 0.0 copy-done.3
  10.9 1.6 copy.36
  12.5 0.0 all-gather.14.cloned.1.call-update
  12.5 0.0 copy-done.5
  12.6 0.1 iota_compare_fusion.1
  12.6 0.0 copy-done.6
  12.7 0.1 multiply_cosine_fusion
  12.8 15.6 %all-gather.6.cloned.1.call-done = bf16[64,8192]{1,0:T(8,128)(2,1)} async-done(((bf16[64,2048]{1,0:T(8,128)(2,1)}), bf16[64,8192]{1,0:T(8,128)(2,1)}) %all-gather.6.cloned.1.call-update) | async-done | bytes 1048592 | tf_op jit(solution)/shard_map/all_gather | solution.py:111
  28.4 1.5 fusion.5
  29.9 0.0 copy-done.4
  29.9 1.5 fusion.7
  31.5 0.0 copy-done
  31.5 1.1 convolution_convert_fusion
  32.6 3.3 all-to-all-start.2
  35.8 2.9 convolution_convert_fusion.1
  38.7 1.0 all-to-all-done.2
  39.7 3.2 all-to-all-start.1
  43.0 3.8 %all-to-all-done.1 = bf16[4,16,128]{2,1,0:T(8,128)(2,1)S(1)} async-done(((bf16[4,16,128]{2,1,0:T(8,128)(2,1)}), bf16[4,16,128]{2,1,0:T(8,128)(2,1)S(1)}, u32[]{:S(2)}, u32[]{:S(2)}) %all-to-all-start.1) | async-done | bytes 16416 | tf_op jit(solution)/shard_map/all_to_all | solution.py:132
  46.8 0.1 subtract_convert_fusion.1
  46.8 63.9 %all-gather.8.cloned.1.call-done = bf16[64,2048,16]{1,2,0:T(8,128)(2,1)} async-done(((bf16[16,2048,16]{1,2,0:T(8,128)(2,1)}), bf16[64,2048,16]{1,2,0:T(8,128)(2,1)}) %all-gather.8.cloned.1.call-update) | async-done | bytes 4194320 | tf_op jit(solution)/shard_map/all_gather | solution.py:69
  110.7 6.7 %fusion.21 = f32[64,16]{0,1:T(8,128)S(1)} fusion(bf16[64,2048,16]{1,2,0:T(8,128)(2,1)} %all-gather.8.cloned.1.call-done, bf16[64,8192]{1,0:T(8,128)(2,1)S(1)} %fusion.7, s32[]{:T(128)S(6)} %select_n.21, pred[64,64]{0,1:T(8,128)(4,1)S(1)} %iota_compare_fusion), kind=kOutput, calls=%fused_computation.22 | convolution fusion | flops 268565504 | bytes 4468740 | tf_op jit(solution)/shard_map/rd,adk->rak/dot_general | solution.py:72
  117.5 7.2 %psum.14 = bf16[64,16]{0,1:T(8,128)(2,1)S(1)} all-reduce(f32[64,16]{0,1:T(8,128)S(1)} %fusion.21), channel_id=1, replica_groups=mesh['groups'=2,'replica'=4,'tensor'=4] {'tensor'}, use_global_device_ids=true, to_apply=%region_2.3 | all-reduce | flops 1024 | bytes 6144 | tf_op jit(solution)/shard_map/psum | solution.py:90
  124.6 32.2 %all-gather.10.cloned.1.call-done = bf16[64,16,1024]{2,0,1:T(8,128)(2,1)} async-done(((bf16[16,16,1024]{2,0,1:T(8,128)(2,1)}), bf16[64,16,1024]{2,0,1:T(8,128)(2,1)}) %all-gather.10.cloned.1.call-update) | async-done | bytes 2097168 | tf_op jit(solution)/shard_map/all_gather | solution.py:78
  156.8 2.1 fusion.19
  158.9 9.7 %fusion.25 = bf16[64,1024]{1,0:T(8,128)(2,1)} fusion(f32[64,1024]{1,0:T(8,128)S(1)} %fusion.19, bf16[64,8192]{1,0:T(8,128)(2,1)S(1)} %fusion.7, bf16[8192,1024]{1,0:T(8,128)(2,1)} %param.16), kind=kOutput, calls=%fused_computation.24 | convolution fusion | flops 1073872896 | bytes 18219008 | tf_op jit(solution)/shard_map/dot_general | solution.py:115
  168.7 3.5 %all-to-all-start = ((bf16[4,16,1024]{2,1,0:T(8,128)(2,1)}), bf16[4,16,1024]{2,1,0:T(8,128)(2,1)S(1)}, u32[]{:S(2)}, u32[]{:S(2)}) async-start(bf16[4,16,1024]{2,1,0:T(8,128)(2,1)} %bitcast.2), calls=%async_computation | async-start | bytes 262144 | tf_op jit(solution)/shard_map/all_to_all | solution.py:131
  172.1 0.2 reduce-scatter.2.cloned.1.call-start
  172.4 0.1 maximum_bitcast_fusion
  172.4 4.3 %all-to-all-done = bf16[4,16,1024]{2,1,0:T(8,128)(2,1)S(1)} async-done(((bf16[4,16,1024]{2,1,0:T(8,128)(2,1)}), bf16[4,16,1024]{2,1,0:T(8,128)(2,1)S(1)}, u32[]{:S(2)}, u32[]{:S(2)}) %all-to-all-start) | async-done | bytes 131104 | tf_op jit(solution)/shard_map/all_to_all | solution.py:131
  176.7 0.9 copy.30
  177.6 1.1 reshape.153
  178.7 0.0 copy-start.7
  178.7 0.1 fusion.37
  178.8 0.3 fusion.45
  179.1 0.0 copy-done.1
  179.1 0.8 fusion.54
  180.0 0.3 fusion.36
  180.3 0.0 copy-done.7
  180.3 0.5 fusion.24
  180.9 7.0 %all_to_all.58 = bf16[16,4,1024]{2,0,1:T(8,128)(2,1)S(1)} all-to-all(bf16[16,4,1024]{2,0,1:T(8,128)(2,1)S(1)} %copy.34), channel_id=1, replica_groups=mesh['groups'=2,'replica'=4,'tensor'=4] {'tensor'}, dimensions={1} | all-to-all | bytes 262144 | tf_op jit(solution)/shard_map/all_to_all | solution.py:136
  187.9 10.2 %fusion.55 = f32[64,8192]{1,0:T(8,128)} fusion(bf16[64,1024]{1,0:T(8,128)(2,1)S(1)} %bitcast.66, bf16[1024,8192]{1,0:T(8,128)(2,1)} %param.19), kind=kOutput, calls=%fused_computation.76 | convolution fusion | flops 1073741824 | bytes 19005440 | tf_op jit(solution)/shard_map/dot_general | solution.py:139
  198.1 0.0 reduce-scatter.2.cloned.1.call-update
  198.1 0.0 copy-start.2
  198.1 4.8 %all-gather.12.cloned.1.call-done = bf16[64,1024,16]{1,2,0:T(8,128)(2,1)} async-done(((bf16[16,1024,16]{1,2,0:T(8,128)(2,1)}), bf16[64,1024,16]{1,2,0:T(8,128)(2,1)}) %all-gather.12.cloned.1.call-update) | async-done | bytes 2097168 | tf_op jit(solution)/shard_map/all_gather | solution.py:69
  202.9 3.9 %fusion.16 = f32[64,16]{0,1:T(8,128)S(1)} fusion(bf16[64,1024,1]{1,0,2:T(8,128)(2,1)S(1)} %bitcast.67, bf16[64,1024,16]{1,2,0:T(8,128)(2,1)} %all-gather.12.cloned.1.call-done, pred[64,64]{0,1:T(8,128)(4,1)S(1)} %iota_compare_fusion), kind=kOutput, calls=%fused_computation.15 | convolution fusion | flops 134347776 | bytes 2236416 | tf_op jit(solution)/shard_map/rd,adk->rak/dot_general | solution.py:72
  206.9 7.0 %psum.15 = bf16[64,16]{0,1:T(8,128)(2,1)S(1)} all-reduce(f32[64,16]{0,1:T(8,128)S(1)} %fusion.16), channel_id=1, replica_groups=mesh['groups'=2,'replica'=4,'tensor'=4] {'tensor'}, use_global_device_ids=true, to_apply=%region_7.8 | all-reduce | flops 1024 | bytes 6144 | tf_op jit(solution)/shard_map/psum | solution.py:90
  213.9 70.0 %all-gather.14.cloned.1.call-done = bf16[64,16,2048]{2,0,1:T(8,128)(2,1)} async-done(((bf16[16,16,2048]{2,0,1:T(8,128)(2,1)}), bf16[64,16,2048]{2,0,1:T(8,128)(2,1)}) %all-gather.14.cloned.1.call-update) | async-done | bytes 4194320 | tf_op jit(solution)/shard_map/all_gather | solution.py:78
  283.8 32.4 %reduce-scatter.2.cloned.1.call-done = f32[64,2048]{1,0:T(8,128)} async-done(((f32[64,8192]{1,0:T(8,128)}), f32[64,2048]{1,0:T(8,128)}) %reduce-scatter.2.cloned.1.call-update) | async-done | bytes 524304 | tf_op jit(solution)/shard_map/reduce_scatter | solution.py:140
  316.2 0.0 copy-done.2
  316.2 3.9 %fusion.4 = bf16[64,2048]{1,0:T(8,128)(2,1)} fusion(bf16[64,16,2048]{2,0,1:T(8,128)(2,1)} %all-gather.14.cloned.1.call-done, f32[64,2048]{1,0:T(8,128)} %reduce-scatter.2.cloned.1.call-done, bf16[64,2048]{1,0:T(8,128)(2,1)S(1)} %copy-done.2, pred[64,64]{0,1:T(8,128)(4,1)S(1)} %iota_compare_fusion, bf16[64,16]{0,1:T(8,128)(2,1)S(1)} %psum.15), kind=kOutput, calls=%fused_computation.7 | convolution fusion | flops 269156352 | bytes 5249024 | tf_op jit(solution)/shard_map/dot_general | solution.py:83
  (14 shorter events, 0.2 us)
Async XLA Ops:
  6.5 24.9 %copy-start = (bf16[8192,128]{1,0:T(8,128)(2,1)S(1)}, bf16[8192,128]{1,0:T(8,128)(2,1)}, u32[]{:S(2)}) copy-start(bf16[8192,128]{1,0:T(8,128)(2,1)} %param.18) | copy-start | bytes 6291460
  6.5 4.3 %copy-start.3 = (bf16[16,16,2048]{2,1,0:T(8,128)(2,1)S(1)}, bf16[16,16,2048]{2,1,0:T(8,128)(2,1)}, u32[]{:S(2)}) copy-start(bf16[16,16,2048]{2,1,0:T(8,128)(2,1)} %param.27) | copy-start | bytes 3145732
  6.5 21.8 %all-gather.6.cloned.1.call-start = ((), (), s32[]{:S(2)}) async-start(), calls=%async_computation.5 | async-start | bytes 1310720 | tf_op jit(solution)/shard_map/all_gather | solution.py:111
  7.3 103.5 %all-gather.8.cloned.1.call-start = ((), (), s32[]{:S(2)}) async-start(), calls=%async_computation.6 | async-start | bytes 5242880 | tf_op jit(solution)/shard_map/all_gather | solution.py:69
  8.0 148.8 %all-gather.10.cloned.1.call-start = ((), (), s32[]{:S(2)}) async-start(), calls=%async_computation.7 | async-start | bytes 2621440 | tf_op jit(solution)/shard_map/all_gather | solution.py:78
  10.2 2.4 copy-start.5
  10.2 2.5 copy-start.6
  10.2 192.7 %all-gather.12.cloned.1.call-start = ((), (), s32[]{:S(2)}) async-start(), calls=%async_computation.9 | async-start | bytes 2621440 | tf_op jit(solution)/shard_map/all_gather | solution.py:69
  10.8 19.1 %copy-start.4 = (f32[8192]{0:T(1024)S(1)}, f32[8192]{0:T(1024)}, u32[]{:S(2)}) copy-start(f32[8192]{0:T(1024)} %param.15) | copy-start | bytes 98308
  10.8 273.0 %all-gather.14.cloned.1.call-start = ((), (), s32[]{:S(2)}) async-start(), calls=%async_computation.10 | async-start | bytes 5242880 | tf_op jit(solution)/shard_map/all_gather | solution.py:78
  32.6 7.1 %all-to-all-start.2 = ((bf16[4,16,128]{2,1,0:T(8,128)(2,1)}), bf16[4,16,128]{2,1,0:T(8,128)(2,1)S(1)}, u32[]{:S(2)}, u32[]{:S(2)}) async-start(bf16[4,16,128]{2,1,0:T(8,128)(2,1)} %bitcast.11), calls=%async_computation.2 | async-start | bytes 32768 | tf_op jit(solution)/shard_map/all_to_all | solution.py:133
  39.7 7.1 %all-to-all-start.1 = ((bf16[4,16,128]{2,1,0:T(8,128)(2,1)}), bf16[4,16,128]{2,1,0:T(8,128)(2,1)S(1)}, u32[]{:S(2)}, u32[]{:S(2)}) async-start(bf16[4,16,128]{2,1,0:T(8,128)(2,1)} %bitcast.6), calls=%async_computation.1 | async-start | bytes 32768 | tf_op jit(solution)/shard_map/all_to_all | solution.py:132
  168.7 10.5 %copy-start.1 = (bf16[16,64,512]{2,1,0:T(8,128)(2,1)S(1)}, bf16[16,64,512]{2,1,0:T(8,128)(2,1)}, u32[]{:S(2)}) copy-start(bf16[16,64,512]{2,1,0:T(8,128)(2,1)} %param.20) | copy-start | bytes 3145732
  168.7 8.1 %all-to-all-start = ((bf16[4,16,1024]{2,1,0:T(8,128)(2,1)}), bf16[4,16,1024]{2,1,0:T(8,128)(2,1)S(1)}, u32[]{:S(2)}, u32[]{:S(2)}) async-start(bf16[4,16,1024]{2,1,0:T(8,128)(2,1)} %bitcast.2), calls=%async_computation | async-start | bytes 262144 | tf_op jit(solution)/shard_map/all_to_all | solution.py:131
  172.1 144.1 %reduce-scatter.2.cloned.1.call-start = ((), (), s32[]{:S(2)}) async-start(), calls=%async_computation.8 | async-start | bytes 2621440 | tf_op jit(solution)/shard_map/reduce_scatter | solution.py:140
  178.7 1.6 copy-start.7
  198.1 118.1 %copy-start.2 = (bf16[64,2048]{1,0:T(8,128)(2,1)S(1)}, bf16[64,2048]{1,0:T(8,128)(2,1)}, u32[]{:S(2)}) copy-start(bf16[64,2048]{1,0:T(8,128)(2,1)} %param.14) | copy-start | bytes 786436
Sparse Core Ops, SparseCore 0:
  8.9 19.4 all-gather.5
  29.9 80.7 all-gather.7
  112.3 44.4 all-gather.9
  158.2 44.6 all-gather.11
  204.4 79.4 all-gather.13
  286.2 29.9 reduce-scatter.1
where the time goes:
time: 328 us; the launch traced here: 327 us
  waiting for transfers between devices  230 us (70%)
  matrix products  42 us (13%)
  blocking collectives  21.2 us (6%)
  between operations  13.7 us (4%)
  starting transfers between devices  10.3 us (3%)
  local copies, waits for them, and re-layouts  5.83 us (2%)
  other arithmetic  3.97 us (1%)
    all_gather x2, waiting for transfers between devices, up_fetch(): piece = lax.all_gather(table, 'replica', axis=0, tiled=True)  102 us
    all_gather x2, waiting for transfers between devices, down_fetch(): piece = lax.all_gather(table, 'replica', axis=0, tiled=True)  68.7 us
    reduce_scatter x1, waiting for transfers between devices, per_device(): lax.psum_scatter(base_projection, 'tensor', scatter_dimension=1, tiled=True)  32.4 us
    all_gather x1, waiting for transfers between devices, per_device(): whole = lax.all_gather(hidden_input, 'tensor', axis=1, tiled=True)  15.6 us
    psum x2, blocking collectives, adapter_contribution(): low = lax.psum(partial_low, 'tensor').astype(jnp.bfloat16)  14.2 us
    dot_general x2, matrix products, down_fetch(): jnp.einsum('rd,adk->rak', act, piece, preferred_element_type=jnp.float32)  10.7 us
    dot_general x1, matrix products, per_device(): jnp.dot(context_local, output_weight, preferred_element_type=jnp.float32)  10.2 us
    dot_general x1, matrix products, per_device(): jnp.dot(normed_hidden, query_weight, preferred_element_type=jnp.float32)  9.73 us
  transfers between devices with their start and end apart: 9, of which 9 were waited for; matrix products, arithmetic and copies ran while one was open for 15% of the time, Pallas kernels for 0%

commit v1 on v0

--- a/solution.py
+++ b/solution.py
@@ -65,30 +65,27 @@
     return context_vectors.astype(jnp.bfloat16).reshape(count, QUERY_HEADS * HEAD_SIZE)
 
 
-def down_fetch(act, table, adapter_index):
-    piece = lax.all_gather(table, "replica", axis=0, tiled=True)
-    count = piece.shape[0]
-    picked = adapter_index[:, None] == jnp.arange(count)[None, :]
-    projected = jnp.einsum("rd,adk->rak", act, piece, preferred_element_type=jnp.float32)
+def local_low(act, table, picked):
+    projected = jnp.einsum("rd,adk->rak", act, table, preferred_element_type=jnp.float32)
     return jnp.sum(jnp.where(picked[:, :, None], projected, 0.0), axis=1)
 
 
-def up_fetch(low, table, adapter_index):
-    rank = table.shape[1]
-    piece = lax.all_gather(table, "replica", axis=0, tiled=True)
-    count = piece.shape[0]
-    picked = adapter_index[:, None] == jnp.arange(count)[None, :]
+def local_up(low, table, picked):
+    count, rank, width = table.shape
     spread = jnp.where(picked[:, :, None], low[:, None, :], jnp.zeros((), jnp.bfloat16))
-    spread = spread.reshape(low.shape[0], count * rank)
     return jnp.dot(
-        spread, piece.reshape(count * rank, piece.shape[2]), preferred_element_type=jnp.float32
+        spread.reshape(low.shape[0], count * rank),
+        table.reshape(count * rank, width),
+        preferred_element_type=jnp.float32,
     )
 
 
-def adapter_contribution(act, table_down, table_up, adapter_index):
-    partial_low = down_fetch(act, table_down, adapter_index)
-    low = lax.psum(partial_low, "tensor").astype(jnp.bfloat16)
-    return up_fetch(low, table_up, adapter_index)
+def adapter_contribution(act, table_down, table_up, picked):
+    rows = lax.all_gather(act, "replica", axis=0, tiled=True)
+    low = lax.psum(local_low(rows, table_down, picked), "tensor").astype(jnp.bfloat16)
+    return lax.psum_scatter(
+        local_up(low, table_up, picked), "replica", scatter_dimension=0, tiled=True
+    )
 
 
 def per_device(
@@ -108,6 +105,10 @@
     output_up_weight,
 ):
     width_local = hidden_input.shape[1]
+    every_index = lax.all_gather(adapter_index, "replica", axis=0, tiled=True)
+    held = query_down_weight.shape[0]
+    mine = lax.axis_index("replica") * held + jnp.arange(held)
+    picked = every_index[:, None] == mine[None, :]
     whole = lax.all_gather(hidden_input, "tensor", axis=1, tiled=True)
     residual_stream = whole.astype(jnp.float32)
     scale = lax.rsqrt(jnp.mean(residual_stream * residual_stream, axis=-1, keepdims=True) + EPSILON)
@@ -125,7 +126,7 @@
     query_vectors = (
         query_base
         + ADAPTER_SCALE
-        * adapter_contribution(normed_portion, query_down_weight, query_up_weight, adapter_index)
+        * adapter_contribution(normed_portion, query_down_weight, query_up_weight, picked)
     ).astype(jnp.bfloat16)
     q_rows, k_rows, v_rows = (
         lax.all_to_all(query_vectors, "tensor", split_axis=0, concat_axis=1, tiled=True),
@@ -139,7 +140,7 @@
     base_projection = jnp.dot(context_local, output_weight, preferred_element_type=jnp.float32)
     base_portion = lax.psum_scatter(base_projection, "tensor", scatter_dimension=1, tiled=True)
     extra_output = adapter_contribution(
-        context_local, output_down_weight, output_up_weight, adapter_index
+        context_local, output_down_weight, output_up_weight, picked
     )
     return (hidden_input.astype(jnp.float32) + base_portion + ADAPTER_SCALE * extra_output).astype(
         jnp.bfloat16

time: 328 us -> 226 us (0.69)
  waiting for transfers between devices: 230 us -> 105 us
  blocking collectives: 21.2 us -> 53.3 us
  matrix products: 42 us -> 32.6 us
    all_gather x4 -> x1, waiting for transfers between devices: 171 us -> 18.2 us  [adapter_contribution(): rows = lax.all_gather(act, 'replica', axis=0, tiled=True)]
    reduce_scatter x0 -> x2, waiting for transfers between devices: none -> 55.7 us  [adapter_contribution(): lax.psum_scatter(local_up(low, table_up, picked), 'replica', scatter_dime...]
    reduce_scatter x1, waiting for transfers between devices: 32.4 us -> 0.02 us  [per_device(): lax.psum_scatter(base_projection, 'tensor', scatter_dimension=1, tiled=True)]
    all_gather x0 -> x1, blocking collectives: none -> 16 us  [adapter_contribution(): rows = lax.all_gather(act, 'replica', axis=0, tiled=True)]
    dot_general x4 -> x2, matrix products: 16.6 us -> 5.36 us  [local_up(): jnp.dot(spread.reshape(low.shape[0], count * rank), table.reshape(count *...]
    unnamed x0 -> x1, blocking collectives: none -> 8.26 us
    psum x2, blocking collectives: 14.2 us -> 21.9 us  [adapter_contribution(): lax.psum(local_low(rows, table_down, picked), 'tensor').astype(jnp.bfloat16)]
    all_gather x1, waiting for transfers between devices: 15.6 us -> 21.1 us  [per_device(): whole = lax.all_gather(hidden_input, 'tensor', axis=1, tiled=True)]
  transfers between devices with their start and end apart: 9 -> 8, of which waited for: 9 -> 7; matrix products, arithmetic and copies ran while one was open for 15% -> 4% of each run, Pallas kernels for 0% -> 0%
where the time goes in v1:
time: 226 us; the launch traced here: 225 us
  waiting for transfers between devices  105 us (46%)
  blocking collectives  53.3 us (24%)
  matrix products  32.6 us (14%)
  between operations  14 us (6%)
  starting transfers between devices  10.1 us (4%)
  other arithmetic  6.11 us (3%)
  local copies, waits for them, and re-layouts  3.65 us (2%)
    reduce_scatter x2, waiting for transfers between devices, adapter_contribution(): lax.psum_scatter(local_up(low, table_up, picked), 'replica', scatter_dime...  55.7 us
    psum x2, blocking collectives, adapter_contribution(): lax.psum(local_low(rows, table_down, picked), 'tensor').astype(jnp.bfloat16)  21.9 us
    all_gather x1, waiting for transfers between devices, per_device(): whole = lax.all_gather(hidden_input, 'tensor', axis=1, tiled=True)  21.1 us
    all_gather x1, waiting for transfers between devices, adapter_contribution(): rows = lax.all_gather(act, 'replica', axis=0, tiled=True)  18.2 us
    all_gather x1, blocking collectives, adapter_contribution(): rows = lax.all_gather(act, 'replica', axis=0, tiled=True)  16 us
    dot_general x1, matrix products, per_device(): jnp.dot(context_local, output_weight, preferred_element_type=jnp.float32)  10.1 us
    dot_general x1, matrix products, per_device(): jnp.dot(normed_hidden, query_weight, preferred_element_type=jnp.float32)  9.45 us
    unnamed x1, blocking collectives  8.26 us
  transfers between devices with their start and end apart: 8, of which 7 were waited for; matrix products, arithmetic and copies ran while one was open for 4% of the time, Pallas kernels for 0%

profile of v1, /device:TPU:0, one launch (start us, length us, event | category | flops | bytes accessed | tf_op | source)
XLA Modules:
  0.0 224.8 jit_solution(17961990904485592726)
XLA Ops:
  6.5 0.0 copy-start
  6.5 0.0 copy-start.7
  6.5 0.0 copy-start.6
  6.5 0.0 all-gather.3.cloned.1.call-start
  6.5 0.7 all-gather.3.cloned.1.call-update
  7.3 0.0 all-gather.5.cloned.1.call-start
  7.3 21.1 %all-gather.3.cloned.1.call-done = bf16[64,8192]{1,0:T(8,128)(2,1)} async-done(((bf16[64,2048]{1,0:T(8,128)(2,1)}), bf16[64,8192]{1,0:T(8,128)(2,1)}) %all-gather.3.cloned.1.call-update) | async-done | bytes 1048592 | tf_op jit(solution)/shard_map/all_gather | solution.py:112
  28.4 1.5 fusion
  29.9 1.5 fusion.2
  31.5 0.7 constant_dynamic-slice_fusion
  32.2 0.0 all-gather.5.cloned.1.call-update
  32.2 0.0 reduce-scatter.4.cloned.1.call-start
  32.3 0.0 copy-done.7
  32.3 0.6 dynamic-slice
  33.6 0.0 copy-done.6
  33.6 0.2 dynamic-update-slice
  33.8 8.3 %all-reduce = s32[256]{0:T(256)S(1)} all-reduce(s32[256]{0:T(256)S(1)} %dynamic-update-slice), channel_id=1, replica_groups=mesh['groups'=2,'replica'=4,'tensor'=4] {'replica'}, use_global_device_ids=true, to_apply=%add | all-reduce | flops 256 | bytes 2048
  42.1 0.1 broadcast_compare_fusion
  42.2 18.2 %all-gather.5.cloned.1.call-done = bf16[256,2048]{1,0:T(8,128)(2,1)} async-done(((bf16[64,2048]{1,0:T(8,128)(2,1)}), bf16[256,2048]{1,0:T(8,128)(2,1)}) %all-gather.5.cloned.1.call-update) | async-done | bytes 1048592 | tf_op jit(solution)/shard_map/all_gather | solution.py:84
  60.3 2.0 fusion.32
  62.4 10.8 %psum.14 = bf16[256,16]{0,1:T(8,128)(2,1)S(1)} all-reduce(f32[256,16]{0,1:T(8,128)S(1)} %select_reduce_fusion.1), channel_id=1, replica_groups=mesh['groups'=2,'replica'=4,'tensor'=4] {'tensor'}, use_global_device_ids=true, to_apply=%region_2.3 | all-reduce | flops 4096 | bytes 24576 | tf_op jit(solution)/shard_map/psum | solution.py:85
  73.2 2.4 %convolution_bitcast_fusion.1 = f32[256,1024]{1,0:T(8,128)} fusion(bf16[16,16,1024]{2,1,0:T(8,128)(2,1)} %param.25, pred[256,16]{0,1:T(8,128)(4,1)S(1)} %broadcast_compare_fusion, bf16[256,16]{0,1:T(8,128)(2,1)S(1)} %psum.14), kind=kOutput, calls=%fused_computation.6 | convolution fusion | flops 134283264 | bytes 1585152 | tf_op jit(solution)/shard_map/dot_general | solution.py:76
  75.5 0.0 reduce-scatter.4.cloned.1.call-update
  75.5 0.0 copy-done.4
  75.6 0.1 iota_compare_fusion
  75.7 0.1 multiply_cosine_fusion
  75.8 0.0 copy-done
  75.8 1.1 convolution_convert_fusion
  76.9 3.3 %all-to-all-start.2 = ((bf16[4,16,128]{2,1,0:T(8,128)(2,1)}), bf16[4,16,128]{2,1,0:T(8,128)(2,1)S(1)}, u32[]{:S(2)}, u32[]{:S(2)}) async-start(bf16[4,16,128]{2,1,0:T(8,128)(2,1)} %bitcast.14), calls=%async_computation.3 | async-start | bytes 32768 | tf_op jit(solution)/shard_map/all_to_all | solution.py:134
  80.1 2.7 %convolution_convert_fusion.1 = bf16[64,128]{1,0:T(8,128)(2,1)} fusion(bf16[64,8192]{1,0:T(8,128)(2,1)S(1)} %fusion.2, bf16[8192,128]{1,0:T(8,128)(2,1)} %param.17), kind=kOutput, calls=%fused_computation.14 | convolution fusion | flops 134225920 | bytes 3162112 | tf_op jit(solution)/shard_map/dot_general | solution.py:117
  82.9 1.1 all-to-all-done.2
  84.0 3.2 %all-to-all-start.1 = ((bf16[4,16,128]{2,1,0:T(8,128)(2,1)}), bf16[4,16,128]{2,1,0:T(8,128)(2,1)S(1)}, u32[]{:S(2)}, u32[]{:S(2)}) async-start(bf16[4,16,128]{2,1,0:T(8,128)(2,1)} %bitcast.9), calls=%async_computation.2 | async-start | bytes 32768 | tf_op jit(solution)/shard_map/all_to_all | solution.py:133
  87.3 3.8 %all-to-all-done.1 = bf16[4,16,128]{2,1,0:T(8,128)(2,1)S(1)} async-done(((bf16[4,16,128]{2,1,0:T(8,128)(2,1)}), bf16[4,16,128]{2,1,0:T(8,128)(2,1)S(1)}, u32[]{:S(2)}, u32[]{:S(2)}) %all-to-all-start.1) | async-done | bytes 16416 | tf_op jit(solution)/shard_map/all_to_all | solution.py:133
  91.0 0.1 subtract_convert_fusion.1
  91.1 10.7 %reduce-scatter.4.cloned.1.call-done = f32[64,1024]{1,0:T(8,128)} async-done(((f32[256,1024]{1,0:T(8,128)}), f32[64,1024]{1,0:T(8,128)}) %reduce-scatter.4.cloned.1.call-update) | async-done | bytes 262160 | tf_op jit(solution)/shard_map/reduce_scatter | solution.py:86
  101.8 9.4 %fusion.5 = bf16[64,1024]{1,0:T(8,128)(2,1)} fusion(bf16[64,8192]{1,0:T(8,128)(2,1)S(1)} %fusion.2, bf16[8192,1024]{1,0:T(8,128)(2,1)} %param.16, f32[64,1024]{1,0:T(8,128)} %reduce-scatter.4.cloned.1.call-done), kind=kOutput, calls=%fused_computation.12 | convolution fusion | flops 1073938432 | bytes 18219008 | tf_op jit(solution)/shard_map/dot_general | solution.py:116
  111.3 3.5 %all-to-all-start = ((bf16[4,16,1024]{2,1,0:T(8,128)(2,1)}), bf16[4,16,1024]{2,1,0:T(8,128)(2,1)S(1)}, u32[]{:S(2)}, u32[]{:S(2)}) async-start(bf16[4,16,1024]{2,1,0:T(8,128)(2,1)} %bitcast.5), calls=%async_computation.1 | async-start | bytes 262144 | tf_op jit(solution)/shard_map/all_to_all | solution.py:132
  114.8 0.0 reduce-scatter.6.cloned.1.call-start
  114.8 0.1 maximum_bitcast_fusion
  114.9 4.5 %all-to-all-done = bf16[4,16,1024]{2,1,0:T(8,128)(2,1)S(1)} async-done(((bf16[4,16,1024]{2,1,0:T(8,128)(2,1)}), bf16[4,16,1024]{2,1,0:T(8,128)(2,1)S(1)}, u32[]{:S(2)}, u32[]{:S(2)}) %all-to-all-start) | async-done | bytes 131104 | tf_op jit(solution)/shard_map/all_to_all | solution.py:132
  119.4 0.9 copy.23
  120.2 1.1 reshape.164
  121.3 0.0 copy-start.5
  121.3 0.1 fusion.11
  121.5 0.3 fusion.23
  121.7 0.0 copy-done.1
  121.8 0.8 fusion.31
  122.6 0.3 fusion.10
  122.9 0.0 copy-done.5
  122.9 0.5 fusion.4
  123.5 7.0 %all_to_all.58 = bf16[16,4,1024]{2,0,1:T(8,128)(2,1)S(1)} all-to-all(bf16[16,4,1024]{2,0,1:T(8,128)(2,1)S(1)} %copy.27), channel_id=1, replica_groups=mesh['groups'=2,'replica'=4,'tensor'=4] {'tensor'}, dimensions={1} | all-to-all | bytes 262144 | tf_op jit(solution)/shard_map/all_to_all | solution.py:137
  130.5 10.1 %fusion.33 = f32[64,8192]{1,0:T(8,128)} fusion(bf16[64,1024]{1,0:T(8,128)(2,1)S(1)} %bitcast.65, bf16[1024,8192]{1,0:T(8,128)(2,1)} %param.19), kind=kOutput, calls=%fused_computation.67 | convolution fusion | flops 1073741824 | bytes 19005440 | tf_op jit(solution)/shard_map/dot_general | solution.py:140
  140.6 0.0 reduce-scatter.6.cloned.1.call-update
  140.7 0.0 reduce-scatter.8.cloned.1.call-start
  140.7 16.0 %all_gather.15 = bf16[256,1024]{1,0:T(8,128)(2,1)S(1)} all-gather(bf16[64,1024]{1,0:T(8,128)(2,1)S(1)} %bitcast.66), channel_id=1, replica_groups=mesh['groups'=2,'replica'=4,'tensor'=4] {'replica'}, dimensions={0}, use_global_device_ids=true | all-gather | bytes 655360 | tf_op jit(solution)/shard_map/all_gather | solution.py:84
  156.8 0.0 copy-done.3
  156.8 0.3 fusion.34
  157.2 11.2 %psum.15 = bf16[256,16]{0,1:T(8,128)(2,1)S(1)} all-reduce(f32[256,16]{0,1:T(8,128)S(1)} %select_reduce_fusion), channel_id=1, replica_groups=mesh['groups'=2,'replica'=4,'tensor'=4] {'tensor'}, use_global_device_ids=true, to_apply=%region_8.9 | all-reduce | flops 4096 | bytes 24576 | tf_op jit(solution)/shard_map/psum | solution.py:85
  168.3 3.0 %convolution_bitcast_fusion = f32[256,2048]{1,0:T(8,128)} fusion(bf16[16,16,2048]{2,1,0:T(8,128)(2,1)} %param.27, pred[256,16]{0,1:T(8,128)(4,1)S(1)} %broadcast_compare_fusion, bf16[256,16]{0,1:T(8,128)(2,1)S(1)} %psum.15), kind=kOutput, calls=%fused_computation | convolution fusion | flops 268500992 | bytes 3158016 | tf_op jit(solution)/shard_map/dot_general | solution.py:76
  171.3 0.0 reduce-scatter.8.cloned.1.call-update
  171.3 0.0 reduce-scatter.6.cloned.1.call-done
  171.4 45.0 %reduce-scatter.8.cloned.1.call-done = f32[64,2048]{1,0:T(8,128)} async-done(((f32[256,2048]{1,0:T(8,128)}), f32[64,2048]{1,0:T(8,128)}) %reduce-scatter.8.cloned.1.call-update) | async-done | bytes 524304 | tf_op jit(solution)/shard_map/reduce_scatter | solution.py:86
  216.3 0.0 copy-done.2
  216.3 2.0 add_convert_fusion
  (19 shorter events, 0.3 us)
Async XLA Ops:
  6.5 69.2 %copy-start = (bf16[8192,128]{1,0:T(8,128)(2,1)S(1)}, bf16[8192,128]{1,0:T(8,128)(2,1)}, u32[]{:S(2)}) copy-start(bf16[8192,128]{1,0:T(8,128)(2,1)} %param.18) | copy-start | bytes 6291460
  6.5 25.8 %copy-start.7 = (u32[32]{0:T(128)S(1)}, u32[32]{0:T(128)}, u32[]{:S(2)}) copy-start(u32[32]{0:T(128)} %constant.44) | copy-start | bytes 388
  6.5 27.0 %copy-start.6 = (s32[64]{0:T(128)S(1)}, s32[64]{0:T(128)}, u32[]{:S(2)}) copy-start(s32[64]{0:T(128)} %param.23) | copy-start | bytes 772
  6.5 21.8 %all-gather.3.cloned.1.call-start = ((), (), s32[]{:S(2)}) async-start(), calls=%async_computation.7 | async-start | bytes 1310720 | tf_op jit(solution)/shard_map/all_gather | solution.py:112
  7.3 53.1 %all-gather.5.cloned.1.call-start = ((), (), s32[]{:S(2)}) async-start(), calls=%async_computation.8 | async-start | bytes 1310720 | tf_op jit(solution)/shard_map/all_gather | solution.py:84
  32.2 69.6 %reduce-scatter.4.cloned.1.call-start = ((), (), s32[]{:S(2)}) async-start(), calls=%async_computation.9 | async-start | bytes 1310720 | tf_op jit(solution)/shard_map/reduce_scatter | solution.py:86
  73.2 2.4 %copy-start.4 = (s32[16]{0:T(128)S(1)}, s32[16]{0:T(128)}, u32[]{:S(2)}) copy-start(s32[16]{0:T(128)} %param.22) | copy-start | bytes 196
  76.9 7.1 %all-to-all-start.2 = ((bf16[4,16,128]{2,1,0:T(8,128)(2,1)}), bf16[4,16,128]{2,1,0:T(8,128)(2,1)S(1)}, u32[]{:S(2)}, u32[]{:S(2)}) async-start(bf16[4,16,128]{2,1,0:T(8,128)(2,1)} %bitcast.14), calls=%async_computation.3 | async-start | bytes 32768 | tf_op jit(solution)/shard_map/all_to_all | solution.py:134
  84.0 7.1 %all-to-all-start.1 = ((bf16[4,16,128]{2,1,0:T(8,128)(2,1)}), bf16[4,16,128]{2,1,0:T(8,128)(2,1)S(1)}, u32[]{:S(2)}, u32[]{:S(2)}) async-start(bf16[4,16,128]{2,1,0:T(8,128)(2,1)} %bitcast.9), calls=%async_computation.2 | async-start | bytes 32768 | tf_op jit(solution)/shard_map/all_to_all | solution.py:133
  111.3 10.5 %copy-start.1 = (bf16[16,64,512]{2,1,0:T(8,128)(2,1)S(1)}, bf16[16,64,512]{2,1,0:T(8,128)(2,1)}, u32[]{:S(2)}) copy-start(bf16[16,64,512]{2,1,0:T(8,128)(2,1)} %param.20) | copy-start | bytes 3145732
  111.3 8.1 %all-to-all-start = ((bf16[4,16,1024]{2,1,0:T(8,128)(2,1)}), bf16[4,16,1024]{2,1,0:T(8,128)(2,1)S(1)}, u32[]{:S(2)}, u32[]{:S(2)}) async-start(bf16[4,16,1024]{2,1,0:T(8,128)(2,1)} %bitcast.5), calls=%async_computation.1 | async-start | bytes 262144 | tf_op jit(solution)/shard_map/all_to_all | solution.py:132
  114.8 56.6 %reduce-scatter.6.cloned.1.call-start = ((), (), s32[]{:S(2)}) async-start(), calls=%async_computation.10 | async-start | bytes 2621440 | tf_op jit(solution)/shard_map/reduce_scatter | solution.py:141
  121.3 1.6 copy-start.5
  140.6 16.1 %copy-start.3 = (bf16[16,1024,16]{1,2,0:T(8,128)(2,1)S(1)}, bf16[16,1024,16]{1,2,0:T(8,128)(2,1)}, u32[]{:S(2)}) copy-start(bf16[16,1024,16]{1,2,0:T(8,128)(2,1)} %param.26) | copy-start | bytes 1572868
  140.7 75.7 %reduce-scatter.8.cloned.1.call-start = ((), (), s32[]{:S(2)}) async-start(), calls=%async_computation.11 | async-start | bytes 2621440 | tf_op jit(solution)/shard_map/reduce_scatter | solution.py:86
  171.3 45.0 %copy-start.2 = (bf16[64,2048]{1,0:T(8,128)(2,1)S(1)}, bf16[64,2048]{1,0:T(8,128)(2,1)}, u32[]{:S(2)}) copy-start(bf16[64,2048]{1,0:T(8,128)(2,1)} %param.14) | copy-start | bytes 786436
Sparse Core Ops, SparseCore 0:
  8.9 19.4 all-gather.2
  32.3 27.9 all-gather.4
  75.7 26.1 reduce-scatter.3
  140.8 29.4 reduce-scatter.5
  172.4 43.8 reduce-scatter.7

commit v2 on v1

v2 whole, which is shorter than its diff:
```python
import functools

import jax
import jax.numpy as jnp
from jax import lax
from jax.experimental import pallas as pl
from jax.experimental.pallas import tpu as pltpu
from jax.sharding import PartitionSpec as P

QUERY_HEADS = 32
KV = 4
HEAD_SIZE = 128
L = 64


ADAPTER_SCALE = 2.0
ROPE_BASE = 500000.0
EPSILON = 1e-05


def rotate(values, position):
    half = values.shape[-1] // 2
    freq = ROPE_BASE ** (-(jnp.arange(half, dtype=jnp.float32) / half))
    angle = position[:, None, None] * freq[None, None, :]
    first = values[..., :half]
    second = values[..., half:]
    cosine = jnp.cos(angle)
    sine = jnp.sin(angle)
    return jnp.concatenate(
        [first * cosine - second * sine, second * cosine + first * sine], axis=-1
    )


def attend(query_vectors, key_new, value_new, key_cache_rows, value_cache_rows, cache_length):
    count = query_vectors.shape[0]
    group = QUERY_HEADS // KV
    position = cache_length.astype(jnp.float32)
    rot_query = rotate(
        query_vectors.astype(jnp.float32).reshape(count, QUERY_HEADS, HEAD_SIZE), position
    ).astype(jnp.bfloat16)
    rotated_key = rotate(
        key_new.astype(jnp.float32).reshape(count, KV, HEAD_SIZE), position
    ).astype(jnp.bfloat16)
    grouped_query = rot_query.reshape(count, KV, group, HEAD_SIZE)
    keys = key_cache_rows.reshape(count, L, KV, HEAD_SIZE)
    values = value_cache_rows.reshape(count, L, KV, HEAD_SIZE)
    softmax_factor = 1.0 / HEAD_SIZE**0.5
    scores = (
        jnp.einsum("bkgd,blkd->bkgl", grouped_query, keys, preferred_element_type=jnp.float32)
        * softmax_factor
    )
    live = jnp.arange(L)[None, :] < cache_length[:, None]
    scores = jnp.where(live[:, None, None, :], scores, -1e30)
    own_scores = (
        jnp.einsum("enxs,ens->enx", grouped_query, rotated_key, preferred_element_type=jnp.float32)
        * softmax_factor
    )
    top = jnp.maximum(jnp.max(scores, axis=-1), own_scores)
    weights = jnp.exp(scores - top[..., None])
    weight_new = jnp.exp(own_scores - top)
    total = jnp.sum(weights, axis=-1) + weight_new
    probs = (weights / total[..., None]).astype(jnp.bfloat16)
    prob_new = (weight_new / total).astype(jnp.bfloat16)
    context_vectors = jnp.einsum(
        "bkgl,blkd->bkgd", probs, values, preferred_element_type=jnp.float32
    )
    fresh = value_new.reshape(count, KV, 1, HEAD_SIZE).astype(jnp.float32)
    context_vectors = context_vectors + prob_new[..., None].astype(jnp.float32) * fresh
    return context_vectors.astype(jnp.bfloat16).reshape(count, QUERY_HEADS * HEAD_SIZE)


MESH = pl.DeviceIdType.MESH
F32 = jnp.float32
BF16 = jnp.bfloat16


def place():
    group, rep, ten = (lax.axis_index(name) for name in ("groups", "replica", "tensor"))

    def peer_r(step, count):
        other = lax.rem(rep + step, count)
        return other, (group, other, ten)

    def peer_t(step, count):
        other = lax.rem(ten + step, count)
        return other, (group, rep, other)

    return rep, ten, peer_r, peer_t


def meet(n_r, n_t, peer_r, peer_t):
    barrier = pltpu.get_barrier_semaphore()
    for step in range(1, n_t):
        pl.semaphore_signal(barrier, inc=1, device_id=peer_t(step, n_t)[1], device_id_type=MESH)
    for step in range(1, n_r):
        pl.semaphore_signal(barrier, inc=1, device_id=peer_r(step, n_r)[1], device_id_type=MESH)
    pl.semaphore_wait(barrier, n_t + n_r - 2)


def remote(src, dst, sems, step, device):
    copy = pltpu.make_async_remote_copy(
        src_ref=src,
        dst_ref=dst,
        send_sem=sems.at[0, step],
        recv_sem=sems.at[1, step],
        device_id=device,
        device_id_type=MESH,
    )
    copy.start()
    return copy


def held_mask(ids, rep, held, rank):
    shape = (held, rank, ids.shape[1])
    owner = lax.broadcasted_iota(jnp.int32, shape, 0) + rep * held
    return jnp.broadcast_to(ids[0:1, :][None], shape) == owner


def low_of(down, rows, ids, rep, held, rank):
    projected = lax.dot_general(down, rows, (((1,), (1,)), ((), ())), preferred_element_type=F32)
    projected = projected.reshape(held, rank, rows.shape[0])
    return jnp.sum(jnp.where(held_mask(ids, rep, held, rank), projected, 0.0), axis=0)


def up_of(low, up, ids, rep, held, rank):
    low = low.astype(BF16).astype(F32)
    shape = (held, rank, ids.shape[1])
    spread = jnp.where(held_mask(ids, rep, held, rank), jnp.broadcast_to(low[None], shape), 0.0)
    spread = spread.reshape(held * rank, ids.shape[1]).T.astype(BF16)
    return jnp.dot(spread, up, preferred_element_type=F32)


def query_kernel(
    n_r, n_t, held, rank,
    hid, gain, ids, down, up, qw_hbm, kw_hbm, vw_hbm,
    q_out, kv_out, ids_out,
    qw, kw, vw, hid_t, hid_z, ids_z, scale_z, nrm, qbase, qbuf, qin, kvbuf, kvin,
    low_own, low_in, con, con_in,
    wsem, s_hid_t, s_hid_z, s_ids, s_scale, s_kv, s_low, s_con, s_q,
):
    rep, ten, peer_r, peer_t = place()
    rows, width = hid.shape
    loads = [
        pltpu.make_async_copy(src, dst, wsem.at[i])
        for i, (src, dst) in enumerate(((kw_hbm, kw), (vw_hbm, vw), (qw_hbm, qw)))
    ]
    for load in loads:
        load.start()
    meet(n_r, n_t, peer_r, peer_t)
    sent = []
    for step in reversed(range(1, n_t)):
        sent.append(remote(hid, hid_t.at[ten], s_hid_t, step, peer_t(step, n_t)[1]))
    for step in range(1, n_r):
        sent.append(remote(ids, ids_z.at[rep], s_ids, step, peer_r(step, n_r)[1]))
    hidden_z = []
    for step in range(1, n_r):
        hidden_z.append(remote(hid, hid_z.at[rep], s_hid_z, step, peer_r(step, n_r)[1]))
    hid_t[ten] = hid[...]
    ids_z[rep] = ids[...]
    for copy in sent:
        copy.wait()
    total = jnp.zeros((rows, 1), F32)
    for t in range(n_t):
        piece = hid_t[t].astype(F32)
        total = total + jnp.sum(piece * piece, axis=-1, keepdims=True)
    scale = lax.rsqrt(total * (1.0 / (n_t * width)) + EPSILON)
    scale_z[rep] = jnp.broadcast_to(scale, (rows, 128))
    scales = []
    for step in range(1, n_r):
        scales.append(
            remote(scale_z.at[rep], scale_z.at[rep], s_scale, step, peer_r(step, n_r)[1])
        )
    for t in range(n_t):
        nrm[t] = (hid_t[t].astype(F32) * scale * gain[t]).astype(BF16)
    low_own[rep] = low_of(down[...], nrm[ten], ids_z[rep], rep, held, rank)

    def project(weight, t):
        part = weight[pl.ds(pl.multiple_of(t * width, width), width), :]
        return jnp.dot(nrm[t], part, preferred_element_type=F32)

    per = rows // n_t
    for which, (load, weight) in enumerate(((loads[0], kw), (loads[1], vw))):
        load.wait()
        acc = project(weight, 0)
        for t in range(1, n_t):
            acc = acc + project(weight, t)
        kvbuf[:, which] = acc.astype(BF16).reshape(n_t, per, weight.shape[1])
    kvs = []
    for step in range(1, n_t):
        other, device = peer_t(step, n_t)
        kvs.append(remote(kvbuf.at[other], kvin.at[ten], s_kv, step, device))
    kvin[ten] = kvbuf[ten]
    loads[2].wait()
    qbase[...] = project(qw, 0)

    @pl.loop(1, n_t)
    def _(t):
        qbase[...] += project(qw, t)

    for step in range(1, n_r):
        hidden_z[step - 1].wait()
        scales[step - 1].wait()
        source = lax.rem(rep - step + n_r, n_r)
        portion = (hid_z[source].astype(F32) * scale_z[source][:, 0:1] * gain[ten]).astype(BF16)
        low_own[source] = low_of(down[...], portion, ids_z[source], rep, held, rank)
    lows = []
    for step in range(1, n_t):
        lows.append(remote(low_own, low_in.at[ten], s_low, step, peer_t(step, n_t)[1]))
    low_in[ten] = low_own[...]
    for copy in lows:
        copy.wait()
    cons = []
    for step in list(range(1, n_r)) + [0]:
        other, device = peer_r(step, n_r)
        low = low_in[0, other]
        for t in range(1, n_t):
            low = low + low_in[t, other]
        con[other] = up_of(low, up[...], ids_z[other], rep, held, rank)
        if step:
            cons.append(remote(con.at[other], con_in.at[rep], s_con, step, device))
    con_in[rep] = con[rep]
    for copy in cons:
        copy.wait()
    extra = con_in[0]
    for j in range(1, n_r):
        extra = extra + con_in[j]
    query = (qbase[...] + ADAPTER_SCALE * extra).astype(BF16)
    qbuf[...] = query.reshape(qbuf.shape)
    qs = []
    for step in range(1, n_t):
        other, device = peer_t(step, n_t)
        qs.append(remote(qbuf.at[other], qin.at[ten], s_q, step, device))
    qin[ten] = qbuf[ten]
    ids_out[...] = ids_z[...]
    for copy in kvs:
        copy.wait()
    kv_out[...] = kvin[...]
    for copy in qs:
        copy.wait()
    q_out[...] = qin[...]


def output_kernel(
    n_r, n_t, held, rank,
    ctx, hid, ids_z, down, up, ow_hbm,
    out,
    ow, ctx_t, ctx_z, base, base_in, low_own, low_in, con, con_in,
    wsem, s_ctx_t, s_ctx_z, s_base, s_low, s_con,
):
    rep, ten, peer_r, peer_t = place()
    rows, width = hid.shape
    load = pltpu.make_async_copy(ow_hbm, ow, wsem.at[0])
    load.start()
    meet(n_r, n_t, peer_r, peer_t)
    sent = []
    for step in range(1, n_t):
        other, device = peer_t(step, n_t)
        sent.append(remote(ctx.at[other], ctx_t.at[ten], s_ctx_t, step, device))
    ctx_t[ten] = ctx[ten]
    for copy in sent:
        copy.wait()
    local = ctx_t[...].reshape(rows, ctx.shape[2])
    ctx_z[rep] = local
    zs = []
    for step in range(1, n_r):
        zs.append(remote(ctx_z.at[rep], ctx_z.at[rep], s_ctx_z, step, peer_r(step, n_r)[1]))
    low_own[rep] = low_of(down[...], local, ids_z[rep], rep, held, rank)
    load.wait()
    bases = []
    for step in list(range(1, n_t)) + [0]:
        other, device = peer_t(step, n_t)
        columns = pl.ds(pl.multiple_of(other * width, width), width)
        base[other] = jnp.dot(ctx_z[rep], ow[:, columns], preferred_element_type=F32)
        if step:
            bases.append(remote(base.at[other], base_in.at[ten], s_base, step, device))
    base_in[ten] = base[ten]
    for step in range(1, n_r):
        zs[step - 1].wait()
        source = lax.rem(rep - step + n_r, n_r)
        low_own[source] = low_of(down[...], ctx_z[source], ids_z[source], rep, held, rank)
    lows = []
    for step in range(1, n_t):
        lows.append(remote(low_own, low_in.at[ten], s_low, step, peer_t(step, n_t)[1]))
    low_in[ten] = low_own[...]
    for copy in lows:
        copy.wait()
    cons = []
    for step in list(range(1, n_r)) + [0]:
        other, device = peer_r(step, n_r)
        low = low_in[0, other]
        for t in range(1, n_t):
            low = low + low_in[t, other]
        con[other] = up_of(low, up[...], ids_z[other], rep, held, rank)
        if step:
            cons.append(remote(con.at[other], con_in.at[rep], s_con, step, device))
    con_in[rep] = con[rep]
    for copy in bases:
        copy.wait()
    total = base_in[0]
    for t in range(1, n_t):
        total = total + base_in[t]
    total = hid[...].astype(F32) + total
    for copy in cons:
        copy.wait()
    extra = con_in[0]
    for j in range(1, n_r):
        extra = extra + con_in[j]
    out[...] = (total + ADAPTER_SCALE * extra).astype(BF16)


VM = pl.BlockSpec(memory_space=pltpu.VMEM)
ANY = pl.BlockSpec(memory_space=pl.ANY)
LIMIT = 54 * 1024 * 1024


def sems(count):
    return pltpu.SemaphoreType.DMA((2, count))


def per_device(
    n_r,
    n_t,
    hidden_input,
    norm_gain_vector,
    query_weight,
    key_weight,
    value_weight,
    output_weight,
    key_cache_rows,
    value_cache_rows,
    cache_length,
    adapter_index,
    query_down_weight,
    query_up_weight,
    output_down_weight,
    output_up_weight,
):
    rows, width = hidden_input.shape
    held, _, rank = query_down_weight.shape
    per = rows // n_t
    q_w, k_w, o_w = query_weight.shape[1], key_weight.shape[1], output_weight.shape[0]

    def flat_down(table):
        return table.transpose(0, 2, 1).reshape(held * rank, table.shape[1])

    def flat_up(table):
        return table.reshape(held * rank, table.shape[2])

    ids = jnp.broadcast_to(adapter_index[None, :], (8, rows))
    q_in, kv_in, ids_z = pl.pallas_call(
        functools.partial(query_kernel, n_r, n_t, held, rank),
        out_shape=(
            jax.ShapeDtypeStruct((n_t, per, q_w), BF16),
            jax.ShapeDtypeStruct((n_t, 2, per, k_w), BF16),
            jax.ShapeDtypeStruct((n_r, 8, rows), jnp.int32),
        ),
        in_specs=[VM] * 5 + [ANY] * 3,
        out_specs=(VM, VM, VM),
        scratch_shapes=[
            pltpu.VMEM(query_weight.shape, BF16),
            pltpu.VMEM(key_weight.shape, BF16),
            pltpu.VMEM(value_weight.shape, BF16),
            pltpu.VMEM((n_t, rows, width), BF16),
            pltpu.VMEM((n_r, rows, width), BF16),
            pltpu.VMEM((n_r, 8, rows), jnp.int32),
            pltpu.VMEM((n_r, rows, 128), F32),
            pltpu.VMEM((n_t, rows, width), BF16),
            pltpu.VMEM((rows, q_w), F32),
            pltpu.VMEM((n_t, per, q_w), BF16),
            pltpu.VMEM((n_t, per, q_w), BF16),
            pltpu.VMEM((n_t, 2, per, k_w), BF16),
            pltpu.VMEM((n_t, 2, per, k_w), BF16),
            pltpu.VMEM((n_r, rank, rows), F32),
            pltpu.VMEM((n_t, n_r, rank, rows), F32),
            pltpu.VMEM((n_r, rows, q_w), F32),
            pltpu.VMEM((n_r, rows, q_w), F32),
            pltpu.SemaphoreType.DMA((3,)),
            sems(n_t), sems(n_r), sems(n_r), sems(n_r), sems(n_t), sems(n_t), sems(n_r), sems(n_t),
        ],
        compiler_params=pltpu.CompilerParams(
            collective_id=0, has_side_effects=True, vmem_limit_bytes=LIMIT
        ),
    )(
        hidden_input,
        norm_gain_vector.reshape(n_t, 1, width),
        ids,
        flat_down(query_down_weight),
        flat_up(query_up_weight),
        query_weight,
        key_weight,
        value_weight,
    )
    q_rows = q_in.transpose(1, 0, 2).reshape(per, n_t * q_w)
    k_rows = kv_in[:, 0].transpose(1, 0, 2).reshape(per, n_t * k_w)
    v_rows = kv_in[:, 1].transpose(1, 0, 2).reshape(per, n_t * k_w)
    context_vectors = attend(q_rows, k_rows, v_rows, key_cache_rows, value_cache_rows, cache_length)
    return pl.pallas_call(
        functools.partial(output_kernel, n_r, n_t, held, rank),
        out_shape=jax.ShapeDtypeStruct((rows, width), BF16),
        in_specs=[VM] * 5 + [ANY],
        out_specs=VM,
        scratch_shapes=[
            pltpu.VMEM(output_weight.shape, BF16),
            pltpu.VMEM((n_t, per, o_w), BF16),
            pltpu.VMEM((n_r, rows, o_w), BF16),
            pltpu.VMEM((n_t, rows, width), F32),
            pltpu.VMEM((n_t, rows, width), F32),
            pltpu.VMEM((n_r, rank, rows), F32),
            pltpu.VMEM((n_t, n_r, rank, rows), F32),
            pltpu.VMEM((n_r, rows, width), F32),
            pltpu.VMEM((n_r, rows, width), F32),
            pltpu.SemaphoreType.DMA((1,)),
            sems(n_t), sems(n_r), sems(n_t), sems(n_t), sems(n_r),
        ],
        compiler_params=pltpu.CompilerParams(
            collective_id=1, has_side_effects=True, vmem_limit_bytes=LIMIT
        ),
    )(
        context_vectors.reshape(per, n_t, o_w).transpose(1, 0, 2),
        hidden_input,
        ids_z,
        flat_down(output_down_weight),
        flat_up(output_up_weight),
        output_weight,
    )


def solution(mesh):
    placed = (
        P(("groups", "replica"), "tensor"),
        P(),
        P(None, "tensor"),
        P(None, "tensor"),
        P(None, "tensor"),
        P("tensor", None),
        P(("groups", "replica", "tensor"), None, None),
        P(("groups", "replica", "tensor"), None, None),
        P(("groups", "replica", "tensor")),
        P(("groups", "replica")),
        P(("groups", "replica"), "tensor", None),
        P(("groups", "replica"), None, "tensor"),
        P(("groups", "replica"), "tensor", None),
        P(("groups", "replica"), None, "tensor"),
    )
    return jax.shard_map(
        functools.partial(per_device, mesh.shape["replica"], mesh.shape["tensor"]),
        mesh=mesh,
        in_specs=placed,
        out_specs=P(("groups", "replica"), "tensor"),
        check_vma=False,
    )
```

time: 226 us -> 158 us (0.70)
  the two profiles are of different devices: /device:TPU:0 before, /device:TPU:26 now
where the time goes in v2:
time: 158 us; the launch traced here: 157 us
  Pallas kernels  148 us (94%)
  other arithmetic  3.99 us (3%)
  local copies, waits for them, and re-layouts  3.96 us (3%)
    pallas_call x1, Pallas kernels, per_device(): pl.pallas_call(functools.partial(output_kernel, n_r, n_t, held, rank), ou...  84.4 us
    pallas_call x1, Pallas kernels, per_device(): pl.pallas_call(functools.partial(query_kernel, n_r, n_t, held, rank), out...  63.3 us

profile of v2, /device:TPU:26, one launch (start us, length us, event | category | flops | bytes accessed | tf_op | source)
XLA Modules:
  0.0 157.2 jit_solution(9547685910709486495)
XLA Ops:
  0.0 0.0 copy-start
  0.0 0.0 copy-start.1
  0.0 0.8 convert_element_type.52
  0.8 0.7 iota_compare_fusion
  1.6 1.2 broadcast_in_dim.11.ids
  2.8 0.1 multiply_cosine_fusion
  2.9 63.3 %shard_map.136 = (bf16[4,16,1024]{2,1,0:T(8,128)(2,1)}, bf16[4,2,16,128]{3,2,1,0:T(8,128)(2,1)}, s32[4,8,64]{2,1,0:T(8,128)}) custom-call(bf16[64,2048]{1,0:T(8,128)(2,1)} %hid.3, f32[4,1,2048]{2,1,0:T(1,128)} %bitcast.57, s32[8,64]{1,0:T(8,128)} %broadcast_in_dim.11.ids, bf16[256,2048]{1,0:T(8,128)(2,1)} %bitcast.50, bf16[256,1024]{1,0:T(8,128)(2,1)} %bitcast.53, ...), custom_call_target="tpu_custom_call" | custom-call | tf_op jit(solution)/shard_map/pallas_call | solution.py:350
  66.2 0.7 convert_bitcast_fusion.2
  67.0 0.1 subtract_convert_fusion.1
  67.1 0.1 maximum_bitcast_fusion
  67.2 0.9 convert_bitcast_fusion
  68.1 0.2 copy.19
  68.3 0.1 reshape.128
  68.4 0.1 fusion.7
  68.5 0.3 fusion.11
  68.8 0.0 copy-done.1
  68.8 0.8 fusion.17
  69.6 0.3 fusion.6
  70.0 0.0 copy-done
  70.0 0.5 fusion.1
  70.5 0.7 copy.42
  71.2 84.4 %shard_map.137 = bf16[64,2048]{1,0:T(8,128)(2,1)} custom-call(bf16[4,16,1024]{2,1,0:T(8,128)(2,1)} %bitcast.52, bf16[64,2048]{1,0:T(8,128)(2,1)} %hid.3, s32[4,8,64]{2,1,0:T(8,128)} %get-tuple-element.10.ids_z, bf16[256,1024]{1,0:T(8,128)(2,1)} %bitcast.54, bf16[256,2048]{1,0:T(8,128)(2,1)} %bitcast.51, bf16[1024,8192]{1,0:T(8,128)(2,1)} %ow_hbm.1), custom_call_target="tpu_custom_call" | custom-call | tf_op jit(solution)/shard_map/pallas_call | solution.py:397
  155.6 1.7 %copy.44 = bf16[64,2048]{1,0:T(8,128)(2,1)} copy(bf16[64,2048]{1,0:T(8,128)(2,1)} %shard_map.137) | data formatting | bytes 524288
  (5 shorter events, 0.1 us)
Async XLA Ops:
  0.0 70.0 %copy-start = (bf16[16,64,512]{2,1,0:T(8,128)(2,1)S(1)}, bf16[16,64,512]{2,1,0:T(8,128)(2,1)}, u32[]{:S(2)}) copy-start(bf16[16,64,512]{2,1,0:T(8,128)(2,1)} %param.21) | copy-start | bytes 3145732
  0.0 68.8 %copy-start.1 = (bf16[16,64,512]{2,1,0:T(8,128)(2,1)S(1)}, bf16[16,64,512]{2,1,0:T(8,128)(2,1)}, u32[]{:S(2)}) copy-start(bf16[16,64,512]{2,1,0:T(8,128)(2,1)} %param.20) | copy-start | bytes 3145732

commit v3 on v2

--- a/solution.py
+++ b/solution.py
@@ -128,6 +128,41 @@
     spread = jnp.where(held_mask(ids, rep, held, rank), jnp.broadcast_to(low[None], shape), 0.0)
     spread = spread.reshape(held * rank, ids.shape[1]).T.astype(BF16)
     return jnp.dot(spread, up, preferred_element_type=F32)
+
+
+def line_sum(n_r, rep, peer_r, con, arrived, sems_line):
+    def hop(side, j, src):
+        step = 1 if side == 0 else n_r - 1
+        return pltpu.make_async_remote_copy(
+            src_ref=src,
+            dst_ref=arrived.at[side, j],
+            send_sem=sems_line.at[side, 0, j],
+            recv_sem=sems_line.at[side, 1, j],
+            device_id=peer_r(step, n_r)[1],
+            device_id_type=MESH,
+        )
+
+    def at_place(i):
+        events = [(n_r - 1 - j + i, 0, j) for j in range(i + 1, n_r)]
+        events += [(j + n_r - 1 - i, 1, j) for j in range(i)]
+        started = []
+        for _, side, j in sorted(events):
+            first = i == (0 if side == 0 else n_r - 1)
+            if not first:
+                hop(side, j, arrived.at[side, j]).wait_recv()
+                arrived[side, j] = arrived[side, j] + con[j]
+            copy = hop(side, j, con.at[j] if first else arrived.at[side, j])
+            copy.start()
+            started.append(copy)
+        for side in range(2):
+            if i != (0 if side == 0 else n_r - 1):
+                hop(side, i, arrived.at[side, i]).wait_recv()
+                con[i] = con[i] + arrived[side, i]
+        for copy in started:
+            copy.wait_send()
+
+    for i in range(n_r):
+        pl.when(rep == i)(functools.partial(at_place, i))
 
 
 def query_kernel(
@@ -209,21 +244,13 @@
     low_in[ten] = low_own[...]
     for copy in lows:
         copy.wait()
-    cons = []
-    for step in list(range(1, n_r)) + [0]:
-        other, device = peer_r(step, n_r)
+    for other in range(n_r):
         low = low_in[0, other]
         for t in range(1, n_t):
             low = low + low_in[t, other]
         con[other] = up_of(low, up[...], ids_z[other], rep, held, rank)
-        if step:
-            cons.append(remote(con.at[other], con_in.at[rep], s_con, step, device))
-    con_in[rep] = con[rep]
-    for copy in cons:
-        copy.wait()
-    extra = con_in[0]
-    for j in range(1, n_r):
-        extra = extra + con_in[j]
+    line_sum(n_r, rep, peer_r, con, con_in, s_con)
+    extra = con[rep]
     query = (qbase[...] + ADAPTER_SCALE * extra).astype(BF16)
     qbuf[...] = query.reshape(qbuf.shape)
     qs = []
@@ -266,13 +293,10 @@
         zs.append(remote(ctx_z.at[rep], ctx_z.at[rep], s_ctx_z, step, peer_r(step, n_r)[1]))
     low_own[rep] = low_of(down[...], local, ids_z[rep], rep, held, rank)
     load.wait()
-    bases = []
     for step in list(range(1, n_t)) + [0]:
-        other, device = peer_t(step, n_t)
+        other, _ = peer_t(step, n_t)
         columns = pl.ds(pl.multiple_of(other * width, width), width)
         base[other] = jnp.dot(ctx_z[rep], ow[:, columns], preferred_element_type=F32)
-        if step:
-            bases.append(remote(base.at[other], base_in.at[ten], s_base, step, device))
     base_in[ten] = base[ten]
     for step in range(1, n_r):
         zs[step - 1].wait()
@@ -281,30 +305,26 @@
     lows = []
     for step in range(1, n_t):
         lows.append(remote(low_own, low_in.at[ten], s_low, step, peer_t(step, n_t)[1]))
+    bases = []
+    for step in range(1, n_t):
+        other, device = peer_t(step, n_t)
+        bases.append(remote(base.at[other], base_in.at[ten], s_base, step, device))
     low_in[ten] = low_own[...]
     for copy in lows:
         copy.wait()
-    cons = []
-    for step in list(range(1, n_r)) + [0]:
-        other, device = peer_r(step, n_r)
+    for other in range(n_r):
         low = low_in[0, other]
         for t in range(1, n_t):
             low = low + low_in[t, other]
         con[other] = up_of(low, up[...], ids_z[other], rep, held, rank)
-        if step:
-            cons.append(remote(con.at[other], con_in.at[rep], s_con, step, device))
-    con_in[rep] = con[rep]
+    line_sum(n_r, rep, peer_r, con, con_in, s_con)
     for copy in bases:
         copy.wait()
     total = base_in[0]
     for t in range(1, n_t):
         total = total + base_in[t]
     total = hid[...].astype(F32) + total
-    for copy in cons:
-        copy.wait()
-    extra = con_in[0]
-    for j in range(1, n_r):
-        extra = extra + con_in[j]
+    extra = con[rep]
     out[...] = (total + ADAPTER_SCALE * extra).astype(BF16)
 
 
@@ -373,9 +393,10 @@
             pltpu.VMEM((n_r, rank, rows), F32),
             pltpu.VMEM((n_t, n_r, rank, rows), F32),
             pltpu.VMEM((n_r, rows, q_w), F32),
-            pltpu.VMEM((n_r, rows, q_w), F32),
+            pltpu.VMEM((2, n_r, rows, q_w), F32),
             pltpu.SemaphoreType.DMA((3,)),
-            sems(n_t), sems(n_r), sems(n_r), sems(n_r), sems(n_t), sems(n_t), sems(n_r), sems(n_t),
+            sems(n_t), sems(n_r), sems(n_r), sems(n_r), sems(n_t), sems(n_t),
+            pltpu.SemaphoreType.DMA((2, 2, n_r)), sems(n_t),
         ],
         compiler_params=pltpu.CompilerParams(
             collective_id=0, has_side_effects=True, vmem_limit_bytes=LIMIT
@@ -408,9 +429,10 @@
             pltpu.VMEM((n_r, rank, rows), F32),
             pltpu.VMEM((n_t, n_r, rank, rows), F32),
             pltpu.VMEM((n_r, rows, width), F32),
-            pltpu.VMEM((n_r, rows, width), F32),
+            pltpu.VMEM((2, n_r, rows, width), F32),
             pltpu.SemaphoreType.DMA((1,)),
-            sems(n_t), sems(n_r), sems(n_t), sems(n_t), sems(n_r),
+            sems(n_t), sems(n_r), sems(n_t), sems(n_t),
+            pltpu.SemaphoreType.DMA((2, 2, n_r)),
         ],
         compiler_params=pltpu.CompilerParams(
             collective_id=1, has_side_effects=True, vmem_limit_bytes=LIMIT

time: 158 us -> 140 us (0.89)
  the two profiles are of different devices: /device:TPU:26 before, /device:TPU:0 now
where the time goes in v3:
time: 140 us; the launch traced here: 139 us
  Pallas kernels  130 us (93%)
  other arithmetic  3.99 us (3%)
  local copies, waits for them, and re-layouts  3.96 us (3%)
  matrix products  1.53 us (1%)
    pallas_call x1, Pallas kernels, per_device(): pl.pallas_call(functools.partial(output_kernel, n_r, n_t, held, rank), ou...  65.8 us
    pallas_call x1, Pallas kernels, per_device(): pl.pallas_call(functools.partial(query_kernel, n_r, n_t, held, rank), out...  64 us

profile of v3, /device:TPU:0, one launch (start us, length us, event | category | flops | bytes accessed | tf_op | source)
XLA Modules:
  0.0 139.4 jit_solution(8453909705480307713)
XLA Ops:
  0.0 0.0 copy-start
  0.0 0.0 copy-start.1
  0.0 0.8 convert_element_type.52
  0.8 0.7 iota_compare_fusion
  1.6 1.2 broadcast_in_dim.11.ids
  2.8 0.1 multiply_cosine_fusion
  2.9 64.0 %shard_map.136 = (bf16[4,16,1024]{2,1,0:T(8,128)(2,1)}, bf16[4,2,16,128]{3,2,1,0:T(8,128)(2,1)}, s32[4,8,64]{2,1,0:T(8,128)}) custom-call(bf16[64,2048]{1,0:T(8,128)(2,1)} %hid.3, f32[4,1,2048]{2,1,0:T(1,128)} %bitcast.57, s32[8,64]{1,0:T(8,128)} %broadcast_in_dim.11.ids, bf16[256,2048]{1,0:T(8,128)(2,1)} %bitcast.50, bf16[256,1024]{1,0:T(8,128)(2,1)} %bitcast.53, ...), custom_call_target="tpu_custom_call" | custom-call | tf_op jit(solution)/shard_map/pallas_call | solution.py:370
  67.0 0.7 convert_bitcast_fusion.2
  67.7 0.1 subtract_convert_fusion.1
  67.8 0.1 maximum_bitcast_fusion
  67.9 0.9 convert_bitcast_fusion
  68.8 0.2 copy.19
  69.0 0.1 reshape.128
  69.1 0.1 fusion.7
  69.3 0.3 fusion.11
  69.5 0.0 copy-done.1
  69.6 0.8 fusion.17
  70.4 0.3 fusion.6
  70.7 0.0 copy-done
  70.7 0.5 fusion.1
  71.2 0.7 copy.42
  71.9 65.8 %shard_map.137 = bf16[64,2048]{1,0:T(8,128)(2,1)} custom-call(bf16[4,16,1024]{2,1,0:T(8,128)(2,1)} %bitcast.52, bf16[64,2048]{1,0:T(8,128)(2,1)} %hid.3, s32[4,8,64]{2,1,0:T(8,128)} %get-tuple-element.10.ids_z, bf16[256,1024]{1,0:T(8,128)(2,1)} %bitcast.54, bf16[256,2048]{1,0:T(8,128)(2,1)} %bitcast.51, bf16[1024,8192]{1,0:T(8,128)(2,1)} %ow_hbm.1), custom_call_target="tpu_custom_call" | custom-call | tf_op jit(solution)/shard_map/pallas_call | solution.py:418
  137.8 1.7 %copy.44 = bf16[64,2048]{1,0:T(8,128)(2,1)} copy(bf16[64,2048]{1,0:T(8,128)(2,1)} %shard_map.137) | data formatting | bytes 524288
  (5 shorter events, 0.1 us)
Async XLA Ops:
  0.0 70.7 %copy-start = (bf16[16,64,512]{2,1,0:T(8,128)(2,1)S(1)}, bf16[16,64,512]{2,1,0:T(8,128)(2,1)}, u32[]{:S(2)}) copy-start(bf16[16,64,512]{2,1,0:T(8,128)(2,1)} %param.21) | copy-start | bytes 3145732
  0.0 69.5 %copy-start.1 = (bf16[16,64,512]{2,1,0:T(8,128)(2,1)S(1)}, bf16[16,64,512]{2,1,0:T(8,128)(2,1)}, u32[]{:S(2)}) copy-start(bf16[16,64,512]{2,1,0:T(8,128)(2,1)} %param.20) | copy-start | bytes 3145732

commit v4 on v3

--- a/solution.py
+++ b/solution.py
@@ -130,7 +130,7 @@
     return jnp.dot(spread, up, preferred_element_type=F32)
 
 
-def line_sum(n_r, rep, peer_r, con, arrived, sems_line):
+def line_sum(n_r, rep, peer_r, make, con, arrived, sems_line):
     def hop(side, j, src):
         step = 1 if side == 0 else n_r - 1
         return pltpu.make_async_remote_copy(
@@ -147,6 +147,7 @@
         events += [(j + n_r - 1 - i, 1, j) for j in range(i)]
         started = []
         for _, side, j in sorted(events):
+            make(j)
             first = i == (0 if side == 0 else n_r - 1)
             if not first:
                 hop(side, j, arrived.at[side, j]).wait_recv()
@@ -154,6 +155,7 @@
             copy = hop(side, j, con.at[j] if first else arrived.at[side, j])
             copy.start()
             started.append(copy)
+        make(i)
         for side in range(2):
             if i != (0 if side == 0 else n_r - 1):
                 hop(side, i, arrived.at[side, i]).wait_recv()
@@ -244,12 +246,13 @@
     low_in[ten] = low_own[...]
     for copy in lows:
         copy.wait()
-    for other in range(n_r):
+    def make(other):
         low = low_in[0, other]
         for t in range(1, n_t):
             low = low + low_in[t, other]
         con[other] = up_of(low, up[...], ids_z[other], rep, held, rank)
-    line_sum(n_r, rep, peer_r, con, con_in, s_con)
+
+    line_sum(n_r, rep, peer_r, make, con, con_in, s_con)
     extra = con[rep]
     query = (qbase[...] + ADAPTER_SCALE * extra).astype(BF16)
     qbuf[...] = query.reshape(qbuf.shape)
@@ -312,12 +315,13 @@
     low_in[ten] = low_own[...]
     for copy in lows:
         copy.wait()
-    for other in range(n_r):
+    def make(other):
         low = low_in[0, other]
         for t in range(1, n_t):
             low = low + low_in[t, other]
         con[other] = up_of(low, up[...], ids_z[other], rep, held, rank)
-    line_sum(n_r, rep, peer_r, con, con_in, s_con)
+
+    line_sum(n_r, rep, peer_r, make, con, con_in, s_con)
     for copy in bases:
         copy.wait()
     total = base_in[0]

time: 140 us -> 139 us (level)
  no operation moved by 1% of the time
where the time goes in v4:
time: 139 us; the launch traced here: 138 us
  Pallas kernels  129 us (93%)
  other arithmetic  3.99 us (3%)
  local copies, waits for them, and re-layouts  3.96 us (3%)
  matrix products  1.53 us (1%)
    pallas_call x1, Pallas kernels, per_device(): pl.pallas_call(functools.partial(output_kernel, n_r, n_t, held, rank), ou...  65.2 us
    pallas_call x1, Pallas kernels, per_device(): pl.pallas_call(functools.partial(query_kernel, n_r, n_t, held, rank), out...  63.5 us

profile of v4, /device:TPU:0, one launch (start us, length us, event | category | flops | bytes accessed | tf_op | source)
XLA Modules:
  0.0 138.3 jit_solution(6475551695016536845)
XLA Ops:
  0.0 0.0 copy-start
  0.0 0.0 copy-start.1
  0.0 0.8 convert_element_type.52
  0.8 0.7 iota_compare_fusion
  1.6 1.2 broadcast_in_dim.11.ids
  2.8 0.1 multiply_cosine_fusion
  2.9 63.5 %shard_map.136 = (bf16[4,16,1024]{2,1,0:T(8,128)(2,1)}, bf16[4,2,16,128]{3,2,1,0:T(8,128)(2,1)}, s32[4,8,64]{2,1,0:T(8,128)}) custom-call(bf16[64,2048]{1,0:T(8,128)(2,1)} %hid.3, f32[4,1,2048]{2,1,0:T(1,128)} %bitcast.57, s32[8,64]{1,0:T(8,128)} %broadcast_in_dim.11.ids, bf16[256,2048]{1,0:T(8,128)(2,1)} %bitcast.50, bf16[256,1024]{1,0:T(8,128)(2,1)} %bitcast.53, ...), custom_call_target="tpu_custom_call" | custom-call | tf_op jit(solution)/shard_map/pallas_call | solution.py:374
  66.4 0.7 convert_bitcast_fusion.2
  67.2 0.1 subtract_convert_fusion.1
  67.3 0.1 maximum_bitcast_fusion
  67.4 0.9 convert_bitcast_fusion
  68.3 0.2 copy.19
  68.5 0.1 reshape.128
  68.6 0.1 fusion.7
  68.7 0.3 fusion.11
  69.0 0.0 copy-done.1
  69.0 0.8 fusion.17
  69.8 0.3 fusion.6
  70.2 0.0 copy-done
  70.2 0.5 fusion.1
  70.7 0.7 copy.42
  71.4 65.2 %shard_map.137 = bf16[64,2048]{1,0:T(8,128)(2,1)} custom-call(bf16[4,16,1024]{2,1,0:T(8,128)(2,1)} %bitcast.52, bf16[64,2048]{1,0:T(8,128)(2,1)} %hid.3, s32[4,8,64]{2,1,0:T(8,128)} %get-tuple-element.10.ids_z, bf16[256,1024]{1,0:T(8,128)(2,1)} %bitcast.54, bf16[256,2048]{1,0:T(8,128)(2,1)} %bitcast.51, bf16[1024,8192]{1,0:T(8,128)(2,1)} %ow_hbm.1), custom_call_target="tpu_custom_call" | custom-call | tf_op jit(solution)/shard_map/pallas_call | solution.py:422
  136.6 1.7 %copy.44 = bf16[64,2048]{1,0:T(8,128)(2,1)} copy(bf16[64,2048]{1,0:T(8,128)(2,1)} %shard_map.137) | data formatting | bytes 524288
  (5 shorter events, 0.1 us)
Async XLA Ops:
  0.0 70.2 %copy-start = (bf16[16,64,512]{2,1,0:T(8,128)(2,1)S(1)}, bf16[16,64,512]{2,1,0:T(8,128)(2,1)}, u32[]{:S(2)}) copy-start(bf16[16,64,512]{2,1,0:T(8,128)(2,1)} %param.21) | copy-start | bytes 3145732
  0.0 69.0 %copy-start.1 = (bf16[16,64,512]{2,1,0:T(8,128)(2,1)S(1)}, bf16[16,64,512]{2,1,0:T(8,128)(2,1)}, u32[]{:S(2)}) copy-start(bf16[16,64,512]{2,1,0:T(8,128)(2,1)} %param.20) | copy-start | bytes 3145732

commit v5 on v4

--- a/solution.py
+++ b/solution.py
@@ -184,14 +184,14 @@
     for load in loads:
         load.start()
     meet(n_r, n_t, peer_r, peer_t)
+    hidden_z = []
+    for step in range(1, n_r):
+        hidden_z.append(remote(hid, hid_z.at[rep], s_hid_z, step, peer_r(step, n_r)[1]))
     sent = []
     for step in reversed(range(1, n_t)):
         sent.append(remote(hid, hid_t.at[ten], s_hid_t, step, peer_t(step, n_t)[1]))
     for step in range(1, n_r):
         sent.append(remote(ids, ids_z.at[rep], s_ids, step, peer_r(step, n_r)[1]))
-    hidden_z = []
-    for step in range(1, n_r):
-        hidden_z.append(remote(hid, hid_z.at[rep], s_hid_z, step, peer_r(step, n_r)[1]))
     hid_t[ten] = hid[...]
     ids_z[rep] = ids[...]
     for copy in sent:

time: 139 us -> 142 us (1.022)
  Pallas kernels: 129 us -> 132 us
    pallas_call x1, Pallas kernels: 63.5 us -> 66.7 us  [per_device(): pl.pallas_call(functools.partial(query_kernel, n_r, n_t, held, rank), out...]
where the time goes in v5:
time: 142 us
  Pallas kernels  132 us (93%)
  other arithmetic  3.99 us (3%)
  local copies, waits for them, and re-layouts  3.96 us (3%)
  matrix products  1.53 us (1%)
    pallas_call x1, Pallas kernels, per_device(): pl.pallas_call(functools.partial(query_kernel, n_r, n_t, held, rank), out...  66.7 us
    pallas_call x1, Pallas kernels, per_device(): pl.pallas_call(functools.partial(output_kernel, n_r, n_t, held, rank), ou...  65.5 us

profile of v5, /device:TPU:0, one launch (start us, length us, event | category | flops | bytes accessed | tf_op | source)
XLA Modules:
  0.0 141.9 jit_solution(4231694193047798288)
XLA Ops:
  0.0 0.0 copy-start
  0.0 0.0 copy-start.1
  0.0 0.8 convert_element_type.52
  0.8 0.7 iota_compare_fusion
  1.6 1.2 broadcast_in_dim.11.ids
  2.8 0.1 multiply_cosine_fusion
  2.9 66.7 %shard_map.136 = (bf16[4,16,1024]{2,1,0:T(8,128)(2,1)}, bf16[4,2,16,128]{3,2,1,0:T(8,128)(2,1)}, s32[4,8,64]{2,1,0:T(8,128)}) custom-call(bf16[64,2048]{1,0:T(8,128)(2,1)} %hid.3, f32[4,1,2048]{2,1,0:T(1,128)} %bitcast.57, s32[8,64]{1,0:T(8,128)} %broadcast_in_dim.11.ids, bf16[256,2048]{1,0:T(8,128)(2,1)} %bitcast.50, bf16[256,1024]{1,0:T(8,128)(2,1)} %bitcast.53, ...), custom_call_target="tpu_custom_call" | custom-call | tf_op jit(solution)/shard_map/pallas_call | solution.py:374
  69.7 0.7 convert_bitcast_fusion.2
  70.4 0.1 subtract_convert_fusion.1
  70.5 0.1 maximum_bitcast_fusion
  70.6 0.9 convert_bitcast_fusion
  71.5 0.2 copy.19
  71.7 0.1 reshape.128
  71.8 0.1 fusion.7
  72.0 0.3 fusion.11
  72.2 0.0 copy-done.1
  72.2 0.8 fusion.17
  73.1 0.3 fusion.6
  73.4 0.0 copy-done
  73.4 0.5 fusion.1
  73.9 0.7 copy.42
  74.6 65.5 %shard_map.137 = bf16[64,2048]{1,0:T(8,128)(2,1)} custom-call(bf16[4,16,1024]{2,1,0:T(8,128)(2,1)} %bitcast.52, bf16[64,2048]{1,0:T(8,128)(2,1)} %hid.3, s32[4,8,64]{2,1,0:T(8,128)} %get-tuple-element.10.ids_z, bf16[256,1024]{1,0:T(8,128)(2,1)} %bitcast.54, bf16[256,2048]{1,0:T(8,128)(2,1)} %bitcast.51, bf16[1024,8192]{1,0:T(8,128)(2,1)} %ow_hbm.1), custom_call_target="tpu_custom_call" | custom-call | tf_op jit(solution)/shard_map/pallas_call | solution.py:422
  140.2 1.7 %copy.44 = bf16[64,2048]{1,0:T(8,128)(2,1)} copy(bf16[64,2048]{1,0:T(8,128)(2,1)} %shard_map.137) | data formatting | bytes 524288
  (5 shorter events, 0.1 us)
Async XLA Ops:
  0.0 73.4 %copy-start = (bf16[16,64,512]{2,1,0:T(8,128)(2,1)S(1)}, bf16[16,64,512]{2,1,0:T(8,128)(2,1)}, u32[]{:S(2)}) copy-start(bf16[16,64,512]{2,1,0:T(8,128)(2,1)} %param.21) | copy-start | bytes 3145732
  0.0 72.2 %copy-start.1 = (bf16[16,64,512]{2,1,0:T(8,128)(2,1)S(1)}, bf16[16,64,512]{2,1,0:T(8,128)(2,1)}, u32[]{:S(2)}) copy-start(bf16[16,64,512]{2,1,0:T(8,128)(2,1)} %param.20) | copy-start | bytes 3145732
